TPU v7x, 32 devices: a whole 2x2x4 slice. The times are simulated.
32 devices in a mesh: space: 8 (over y, x, core), slot: 4 (over z).
Axes of the slice: x: 2, y: 2, z: 4, core: 2. Of those that a mesh axis runs over, the one named last changes fastest.
Arguments:
- window_values: bfloat16 [16384, 8192], P('space', 'slot'), may hold values from -4 to 4
- window_scales: bfloat16 [128, 8192], P('space', 'slot'), may hold values from 0.049804688 to 1
- slab_values: bfloat16 [16384, 512], P('space', 'slot'), may hold values from -4 to 4
- slab_scales: bfloat16 [128, 512], P('space', 'slot'), may hold values from 0.049804688 to 1
- test_matrix: bfloat16 [8192, 256], P('slot'), may hold values from -1 to 1
- owner_slot: int32 [4], replicated, may hold values from 0 to 3, each once
- offset: int32 [1], replicated, may hold values from 0 to 1536
Outputs:
- pod_basis: bfloat16 [16384, 256], P('space')
- pod_coefs: float32 [256, 8192], P(None, 'slot')
All inputs are finite; a program needn't handle non-finite values.
Results may differ from a plain program's by a relative error of at most 0.0049.
Values may be sent and summed in bfloat16 or wider, within the bound.
A program may use at most 128 MiB of HBM per device.

v0:
```python
import jax
import jax.numpy as jnp
from jax import lax
from jax.sharding import PartitionSpec as P

SLAB = 512
BLOCK = 128


def expand(values, scales):
    row_count, col_count = values.shape
    scaled = (
        values.astype(jnp.float32).reshape(row_count // BLOCK, BLOCK, col_count)
        * scales.astype(jnp.float32)[:, None, :]
    )
    return scaled.reshape(row_count, col_count).astype(jnp.bfloat16)


def factor(gram_matrix, cell_count):
    lower_factor = jnp.linalg.cholesky(gram_matrix / cell_count)
    identity = jnp.eye(gram_matrix.shape[0], dtype=jnp.float32)
    return lax.linalg.triangular_solve(lower_factor, identity, left_side=True, lower=True)


def gram_of(sketch):
    return lax.dot_general(
        sketch,
        sketch,
        (((0,), (0,)), ((), ())),
        precision=lax.Precision.HIGHEST,
        preferred_element_type=jnp.float32,
    )


def inner_rows(left, right):
    return lax.dot_general(
        left,
        right,
        (((0,), (0,)), ((), ())),
        precision=lax.Precision.HIGHEST,
        preferred_element_type=jnp.float32,
    )


def apply_left(inverse, matrix):
    return jnp.dot(
        inverse, matrix, precision=lax.Precision.HIGHEST, preferred_element_type=jnp.float32
    )


def local(window_values, window_scales, slab_values, slab_scales, test_matrix, owner_slot, offset):
    rows_here = window_values.shape[0]
    total_rows = rows_here * lax.axis_size("space")
    slot_here = lax.axis_index("slot")
    is_owner = slot_here == owner_slot[0]
    first_col = offset[0]
    slab_whole, scales_whole = (
        lax.all_gather(slab_values, "slot", axis=1, tiled=True),
        lax.all_gather(slab_scales, "slot", axis=1, tiled=True),
    )
    current_values = lax.dynamic_slice_in_dim(window_values, first_col, SLAB, 1)
    current_scales = lax.dynamic_slice_in_dim(window_scales, first_col, SLAB, 1)
    merged_values = lax.dynamic_update_slice_in_dim(
        window_values, jnp.where(is_owner, slab_whole, current_values), first_col, 1
    )
    merged_scales = lax.dynamic_update_slice_in_dim(
        window_scales, jnp.where(is_owner, scales_whole, current_scales), first_col, 1
    )
    window = expand(merged_values, merged_scales)
    sketch = lax.psum(jnp.dot(window, test_matrix, preferred_element_type=jnp.float32), "slot")
    cross = inner_rows(sketch, window)
    gram_matrix, cross_total = lax.psum((gram_of(sketch), cross), "space")
    inverse = factor(gram_matrix, total_rows)
    coef_window = apply_left(inverse, cross_total)
    pod_basis = jnp.dot(
        sketch, inverse.T, precision=lax.Precision.HIGHEST, preferred_element_type=jnp.float32
    ).astype(jnp.bfloat16)
    return (pod_basis, coef_window / jnp.sqrt(jnp.float32(total_rows)))


def solution(mesh):
    return jax.shard_map(
        local,
        mesh=mesh,
        in_specs=(
            P("space", "slot"),
            P("space", "slot"),
            P("space", "slot"),
            P("space", "slot"),
            P("slot", None),
            P(),
            P(),
        ),
        out_specs=(P("space", None), P(None, "slot")),
        check_vma=False,
    )
```

profile of v0, /device:TPU:0, one launch (start us, length us, event | category | flops | bytes accessed | tf_op | source)
XLA Modules:
  0.0 358.7 jit_solution(3392306028680638692)
XLA Ops:
  7.3 8.3 %copy.31 = bf16[2048,2048]{1,0:T(8,128)(2,1)} copy(bf16[2048,2048]{1,0:T(8,128)(2,1)} %param.7) | data formatting | bytes 16777216
  16.4 13.6 %all_gather.7 = bf16[16,512]{1,0:T(8,128)(2,1)S(1)} all-gather(bf16[16,128]{1,0:T(8,128)(2,1)S(1)} %copy-done.5), channel_id=1, replica_groups=mesh['space'=8,'slot'=4] {'slot'}, dimensions={1}, use_global_device_ids=true | all-gather | bytes 20480 | tf_op jit(solution)/shard_map/all_gather | solution.py:59
  30.5 34.2 %all-gather.2.cloned.1.call-done = bf16[2048,512]{1,0:T(8,128)(2,1)} async-done(((bf16[2048,128]{1,0:T(8,128)(2,1)}), bf16[2048,512]{1,0:T(8,128)(2,1)}) %all-gather.2.cloned.1.call-update) | async-done | bytes 2097168 | tf_op jit(solution)/shard_map/all_gather | solution.py:58
  64.7 3.1 dynamic-slice_select_fusion
  67.9 21.1 %dynamic_update_slice.6 = bf16[2048,2048]{1,0:T(8,128)(2,1)} dynamic-update-slice(bf16[2048,2048]{1,0:T(8,128)(2,1)} %copy.31, bf16[2048,512]{1,0:T(8,128)(2,1)S(1)} %dynamic-slice_select_fusion, s32[]{:T(128)} %copy.33, s32[]{:T(128)S(6)} %select_n.27) | dynamic-update-slice | bytes 4194308 | tf_op jit(solution)/shard_map/dynamic_update_slice | solution.py:63
  89.0 9.7 %fusion = bf16[2048,2048]{1,0:T(8,128)(2,1)} fusion(bf16[2048,2048]{1,0:T(8,128)(2,1)} %dynamic_update_slice.6, f32[16,2048]{1,0:T(8,128)S(1)} %convert_element_type.14), kind=kLoop, calls=%fused_computation.3 | loop fusion | flops 12582912 | bytes 16908288 | tf_op jit(solution)/shard_map/convert_element_type | solution.py:16
  98.7 7.1 %fusion.12 = f32[2048,256]{1,0:T(8,128)} fusion(bf16[2048,2048]{1,0:T(8,128)(2,1)} %fusion, bf16[2048,256]{1,0:T(8,128)(2,1)S(1)} %copy-done), kind=kOutput, calls=%fused_computation.39 | convolution fusion | flops 2147483648 | bytes 11534336 | tf_op jit(solution)/shard_map/dot_general | solution.py:70
  105.9 85.5 %all-reduce.5.cloned.1.call-done = f32[2048,256]{1,0:T(8,128)} async-done(((f32[2048,256]{1,0:T(8,128)}), f32[2048,256]{1,0:T(8,128)}) %all-reduce.5.cloned.1.call-update) | async-done | bytes 2097168 | tf_op jit(solution)/shard_map/psum | solution.py:70
  191.3 11.8 %fusion.14 = f32[256,2048]{1,0:T(8,128)} fusion(f32[2048,256]{1,0:T(8,128)} %all-reduce.5.cloned.1.call-done, bf16[2048,2048]{1,0:T(8,128)(2,1)} %fusion), kind=kOutput, calls=%fused_computation.41 | convolution fusion | flops 12884901888 | bytes 12582912 | tf_op jit(solution)/shard_map/dot_general | solution.py:36
  203.1 4.2 %fusion.13 = f32[256,256]{0,1:T(8,128)} fusion(f32[2048,256]{1,0:T(8,128)S(1)} %copy-done.1), kind=kOutput, calls=%fused_computation.40 | convolution fusion | flops 1610612736 | bytes 2359296 | tf_op jit(solution)/shard_map/dot_general | solution.py:26
  207.4 62.1 %all-reduce.7.cloned.1.call-done = (f32[256,256]{0,1:T(8,128)}, f32[256,2048]{1,0:T(8,128)}) async-done(((f32[256,256]{0,1:T(8,128)}, f32[256,2048]{1,0:T(8,128)}), (f32[256,256]{0,1:T(8,128)}, f32[256,2048]{1,0:T(8,128)})) %all-reduce.7.cloned.1.call-update) | async-done | bytes 2359312 | tf_op jit(solution)/shard_map/psum | solution.py:72
  269.5 1.7 broadcast_multiply_fusion
  273.9 11.7 %cholesky.50 = f32[128,128]{1,0:T(8,128)S(1)} custom-call(f32[128,128]{1,0:T(8,128)S(1)} %cholesky.118), custom_call_target="Cholesky" | custom-call | tf_op jit(solution)/shard_map/jit(cholesky)/cholesky | solution.py:20
  286.3 10.6 %custom-call.14 = f32[1,128,128]{1,2,0:T(8,128)S(1)} custom-call(f32[1,128,128]{2,1,0:T(8,128)} %get-tuple-element.25), custom_call_target="InvertDiagBlocksLowerTriangular" | custom-call | tf_op jit(solution)/shard_map/jit(cholesky)/cholesky | solution.py:20
  298.0 1.7 convolution_subtract_fusion.1
  299.8 12.8 %cholesky.105 = f32[128,128]{1,0:T(8,128)S(1)} custom-call(f32[128,128]{1,0:T(8,128)} %convolution_subtract_fusion.1), custom_call_target="Cholesky" | custom-call | tf_op jit(solution)/shard_map/jit(cholesky)/cholesky | solution.py:20
  315.7 5.2 %while.1 = (s32[]{:T(128)}, f32[256,256]{1,0:T(8,128)S(1)}, s32[2,2]{1,0:T(2,128)S(1)}, f32[2,128,128]{2,1,0:T(8,128)}, s32[]{:T(128)}) while((s32[]{:T(128)}, f32[256,256]{1,0:T(8,128)S(1)}, s32[2,2]{1,0:T(2,128)S(1)}, f32[2,128,128]{2,1,0:T(8,128)}, s32[]{:T(128)}) %tuple.27), condition=%wide.while_cond, body=%wide.while_body.sunk | while | flops 2 | bytes 132705 | solution.py:22
  316.3 2.0 bitcast_dynamic-update-slice_fusion.2
  318.9 2.0 bitcast_dynamic-update-slice_fusion.2
  320.9 21.1 %custom-call.15 = f32[2,128,128]{1,2,0:T(8,128)} custom-call(f32[2,128,128]{2,1,0:T(8,128)} %get-tuple-element.9), custom_call_target="InvertDiagBlocksLowerTriangular" | custom-call | tf_op jit(solution)/shard_map/triangular_solve | solution.py:22
  342.0 1.1 fusion.2
  343.4 1.2 fusion.5
  344.5 4.8 %convolution_multiply_fusion = f32[256,2048]{1,0:T(8,128)} fusion(f32[256,2048]{1,0:T(8,128)} %get-tuple-element.19, f32[128,256]{1,0:T(8,128)S(1)} %fusion.5, f32[128,256]{1,0:T(8,128)S(1)} %fusion.2), kind=kOutput, calls=%fused_computation.4 | convolution fusion | flops 1611202560 | bytes 4456448 | tf_op jit(solution)/shard_map/dot_general | solution.py:46
  349.3 2.8 convolution_convert_fusion
  (42 shorter events, 8.5 us)
Async XLA Ops:
  7.2 91.6 %copy-start = (bf16[2048,256]{1,0:T(8,128)(2,1)S(1)}, bf16[2048,256]{1,0:T(8,128)(2,1)}, u32[]{:S(2)}) copy-start(bf16[2048,256]{1,0:T(8,128)(2,1)} %param.11) | copy-start | bytes 3145732
  7.2 8.4 %copy-start.4 = (bf16[16,2048]{1,0:T(8,128)(2,1)S(1)}, bf16[16,2048]{1,0:T(8,128)(2,1)}, u32[]{:S(2)}) copy-start(bf16[16,2048]{1,0:T(8,128)(2,1)} %param.8) | copy-start | bytes 196612
  7.2 9.2 %copy-start.5 = (bf16[16,128]{1,0:T(8,128)(2,1)S(1)}, bf16[16,128]{1,0:T(8,128)(2,1)}, u32[]{:S(2)}) copy-start(bf16[16,128]{1,0:T(8,128)(2,1)} %param.10) | copy-start | bytes 12292
  7.2 9.1 %copy-start.6 = (s32[4]{0:T(128)S(1)}, s32[4]{0:T(128)}, u32[]{:S(2)}) copy-start(s32[4]{0:T(128)} %param.12) | copy-start | bytes 52
  7.2 57.5 %all-gather.2.cloned.1.call-start = ((), (), s32[]{:S(2)}) async-start(), calls=%async_computation | async-start | bytes 2621440 | tf_op jit(solution)/shard_map/all_gather | solution.py:58
  15.6 175.7 %all-reduce.5.cloned.1.call-start = ((), (), s32[]{:S(2)}) async-start(), calls=%async_computation.1 | async-start | bytes 4194304 | tf_op jit(solution)/shard_map/psum | solution.py:70
  105.8 163.7 %all-reduce.7.cloned.1.call-start = ((), (), s32[]{:S(2)}) async-start(), calls=%async_computation.2 | async-start | bytes 4718592 | tf_op jit(solution)/shard_map/psum | solution.py:72
  191.3 11.8 %copy-start.1 = (f32[2048,256]{1,0:T(8,128)S(1)}, f32[2048,256]{1,0:T(8,128)}, u32[]{:S(2)}) copy-start(f32[2048,256]{1,0:T(8,128)} %all-reduce.5.cloned.1.call-done) | copy-start | bytes 6291460
  273.2 0.7 copy-start.3
  312.6 2.0 copy-start.2
Sparse Core Ops, SparseCore 0:
  15.8 48.9 all-gather.1
  105.9 85.3 all-reduce.4
  207.4 61.9 all-reduce.6
where the time goes:
time: 360 us; the launch traced here: 359 us
  waiting for transfers between devices  182 us (51%)
  other arithmetic  74.2 us (21%)
  local copies, waits for them, and re-layouts  37 us (10%)
  matrix products  35.9 us (10%)
  between operations  16 us (4%)
  blocking collectives  13.6 us (4%)
    psum x1, waiting for transfers between devices, local(): lax.psum(jnp.dot(window, test_matrix, preferred_element_type=jnp.float32)...  85.5 us
    psum x1, waiting for transfers between devices, local(): gram_matrix, cross_total = lax.psum((gram_of(sketch), cross), 'space')  62.1 us
    another operation x6, other arithmetic, factor(): lower_factor = jnp.linalg.cholesky(gram_matrix / cell_count)  36.5 us
    all_gather x1, waiting for transfers between devices, local(): lax.all_gather(slab_values, 'slot', axis=1, tiled=True)  34.2 us
    another operation x3, other arithmetic, factor(): lax.linalg.triangular_solve(lower_factor, identity, left_side=True, lower...  22.1 us
    dynamic_update_slice x1, local copies, waits for them, and re-layouts, local(): lax.dynamic_update_slice_in_dim(window_values, jnp.where(is_owner, slab_w...  21.1 us
    all_gather x1, blocking collectives, local(): lax.all_gather(slab_scales, 'slot', axis=1, tiled=True)  13.6 us
    dot_general x1, matrix products, inner_rows(): lax.dot_general(left, right, (((0,), (0,)), ((), ())), precision=lax.Prec...  11.8 us
  transfers between devices with their start and end apart: 3, of which 3 were waited for; matrix products, arithmetic and copies ran while one was open for 0% of the time, Pallas kernels for 0%

commit v1 on v0

v1 whole, which is shorter than its diff:
```python
import functools

import jax
import jax.numpy as jnp
from jax import lax
from jax.experimental import pallas as pl
from jax.experimental.pallas import tpu as pltpu
from jax.sharding import PartitionSpec as P

MESH = pl.DeviceIdType.MESH
F32, BF16 = jnp.float32, jnp.bfloat16
SUB = 2


def dot(a, b, contract=((1,), (0,))):
    return lax.dot_general(a, b, (contract, ((), ())), preferred_element_type=F32)


def dot_full(a, b, contract=((1,), (0,))):
    return lax.dot_general(
        a, b, (contract, ((), ())), precision=lax.Precision.HIGHEST, preferred_element_type=F32
    )


def split(x):
    hi = x.astype(BF16)
    return hi, (x - hi.astype(F32)).astype(BF16)


def inverse_lower(t_ref, size, between):
    row = lax.broadcasted_iota(jnp.int32, (size, size), 0)
    lane = lax.broadcasted_iota(jnp.int32, (size, size), 1)
    sub8 = lax.broadcasted_iota(jnp.int32, (8, size), 0)
    lane8 = lax.broadcasted_iota(jnp.int32, (8, size), 1)
    lane1 = lax.broadcasted_iota(jnp.int32, (1, size), 1)

    def round_of(g, _):
        t = t_ref[...]
        tile = t_ref[pl.ds(pl.multiple_of(g * 8, 8), 8), :]
        for s in range(8):
            below = row > g * 8 + s
            below8 = sub8 > s
            r = tile[s : s + 1, :]
            inv = 1.0 / tile[s : s + 1, s : s + 1]
            r = jnp.where(lane1 == s, 1.0, r) * inv
            col8 = jnp.where(below8, tile[:, s : s + 1], 0.0)
            tile = jnp.where(below8 & (lane8 == s), 0.0, tile) - col8 * r
            col = jnp.where(below, t[:, s : s + 1], 0.0)
            t = jnp.where(below & (lane == s), 0.0, t) - col * r
        t_ref[...] = pltpu.roll(t, size - 8, 1)
        return 0

    rounds = size // 8
    parts = len(between) + 1
    edges = [rounds * i // parts for i in range(parts + 1)]
    for i in range(parts):
        lax.fori_loop(edges[i], edges[i + 1], round_of, 0)
        if i < len(between):
            between[i]()
    t = t_ref[...]
    pivot = jnp.sum(jnp.where(row == lane, t, 0.0), axis=1, keepdims=True)
    unit = jnp.where(row > lane, t, jnp.where(row == lane, 1.0, 0.0))
    return unit * lax.rsqrt(pivot)


def kernel(
    n, nsp,
    vals, scales, slab, slab_sc, test, owner, offset,
    basis_o, coef_o,
    win, win_s, msc, place, tm_out, tm_in, part, rs_out, rs_in, sk, skt,
    gr, g_out, g_in, g_fin, cr, c_out, c_in, c_fin, sl_in, t_ref, inv_ref,
    tm_ss, tm_rs, rr_ss, rr_rs, rl_ss, rl_rs, ar_ss, ar_rs, al_ss, al_rs,
    g_ss, g_rs, c_ss, c_rs, sl_ss, sl_rs,
):
    z = lax.axis_index("slot")
    me = lax.axis_index("space")
    core = lax.rem(me, 2)
    rows, cols = vals.shape
    rank = test.shape[1]
    block = rows // scales.shape[0]
    sc = slab.shape[1]
    sw = sl_in.shape[2]
    nb = nsp.bit_length() - 1
    half = rank // 2
    chunk = rows // n
    sub = chunk // SUB
    total_rows = rows * nsp

    strides = [jnp.int32(1)]
    for i in range(1, nb):
        strides.append((1 << i) * (1 - core) + (1 << (nb - i)) * core)
    strides.append(jnp.int32(1))

    def partner(stride):
        return me + stride * (1 - 2 * lax.rem(me // stride, 2))

    def copy(src, dst, ss, rs, space=None, slot=None):
        return pltpu.make_async_remote_copy(
            src_ref=src, dst_ref=dst, send_sem=ss, recv_sem=rs,
            device_id={"space": me if space is None else space, "slot": z if slot is None else slot},
            device_id_type=MESH,
        )

    barrier = pltpu.get_barrier_semaphore()
    for d in range(1, n):
        pl.semaphore_signal(
            barrier, inc=1, device_id={"space": me, "slot": lax.rem(z + d, n)}, device_id_type=MESH
        )
    for i in range(nb):
        pl.semaphore_signal(
            barrier, inc=1, device_id={"space": partner(jnp.int32(1 << i)), "slot": z}, device_id_type=MESH
        )

    first = jnp.where(owner[0] == z, offset[0], -(2 ** 20))

    @pl.loop(0, n)
    def _(s):
        diff = lax.broadcasted_iota(jnp.int32, (sc, cols), 1) - lax.broadcasted_iota(
            jnp.int32, (sc, cols), 0
        )
        one_hot = jnp.where(diff == first + s * sc, 1.0, 0.0).astype(BF16)
        place[pl.ds(pl.multiple_of(s * sc, sc), sc), :] = one_hot
        tm_out[s] = dot(one_hot, test[...]).astype(BF16)

    pl.semaphore_wait(barrier, n - 1 + nb)

    def tm_copy(d):
        peer = lax.rem(z + d, n)
        return copy(tm_out.at[peer], tm_in.at[d], tm_ss.at[d], tm_rs.at[d], slot=peer)

    for d in range(1, n):
        tm_copy(d).start()

    col = lax.broadcasted_iota(jnp.int32, scales.shape, 1) - first
    replaced = (col >= 0) & (col < n * sc)
    msc[...] = jnp.where(replaced, 0.0, scales[...].astype(F32))

    ssc = slab_sc[...].astype(F32)
    for b in range(rows // block):
        win_s[b * block : (b + 1) * block, :] = (
            slab[b * block : (b + 1) * block, :].astype(F32) * ssc[b : b + 1, :]
        ).astype(BF16)

    @pl.loop(0, rows // block)
    def _(b):
        at = pl.ds(pl.multiple_of(b * block, block), block)
        w = (vals[at, :].astype(F32) * msc[pl.ds(b, 1), :]).astype(BF16)
        win[at, :] = w
        part[at, :] = dot(w, test[...])

    rows_new = tm_out[z].astype(F32)
    for d in range(1, n):
        tm_copy(d).wait_recv()
        rows_new += tm_in[d].astype(F32)
    rows_new = rows_new.astype(BF16)

    @pl.loop(0, n)
    def _(c):
        at = pl.ds(pl.multiple_of(c * chunk, chunk), chunk)
        part[at, :] += dot(win_s[at, :], rows_new)

    def span(c, h):
        return pl.ds(pl.multiple_of(c * chunk + h * sub, sub), sub)

    def rs_copy(way, c, h):
        ss, rs = ((rr_ss, rr_rs), (rl_ss, rl_rs))[way]
        step = 1 - 2 * way
        at = span(c, h)
        return copy(
            rs_out.at[way, at], rs_in.at[way, at], ss.at[c, h], rs.at[c, h], slot=z + step
        )

    has = (z > 0, z < n - 1)
    for d in range(n - 1, 0, -1):
        for h in range(SUB):
            for way in (0, 1):
                c = z + d * (1 - 2 * way)

                @pl.when((c >= 0) & (c < n))
                def _():
                    at = span(c, h)

                    @pl.when(has[way])
                    def _():
                        rs_copy(way, c, h).wait_recv()
                        part[at, :] += rs_in[way, at, :].astype(F32)

                    rs_out[way, at, :] = part[at, :].astype(BF16)
                    rs_copy(way, c, h).start()

    def ag_copy(way, c, h):
        ss, rs = ((ar_ss, ar_rs), (al_ss, al_rs))[way]
        at = span(c, h)
        return copy(sk.at[at], sk.at[at], ss.at[c, h], rs.at[c, h], slot=z + 1 - 2 * way)

    for h in range(SUB):
        at = span(z, h)
        for way in (0, 1):

            @pl.when(has[way])
            def _():
                rs_copy(way, z, h).wait_recv()
                part[at, :] += rs_in[way, at, :].astype(F32)

        sk[at, :] = part[at, :].astype(BF16)
        for way in (0, 1):

            @pl.when(has[1 - way])
            def _():
                ag_copy(way, z, h).start()

    for d in range(1, n):
        for h in range(SUB):
            for way in (0, 1):
                c = z - d * (1 - 2 * way)

                @pl.when((c >= 0) & (c < n))
                def _():
                    ag_copy(way, c, h).wait_recv()

                    @pl.when(has[1 - way])
                    def _():
                        ag_copy(way, c, h).start()

    @pl.loop(0, n)
    def _(c):
        at = pl.ds(pl.multiple_of(c * chunk, chunk), chunk)
        skt[:, at] = sk[at, :].astype(F32).T.astype(BF16)

    def half_at(c):
        return pl.ds(pl.multiple_of(c * half, half), half)

    def g_copy(i):
        if i == 0:
            return copy(gr.at[half_at(1 - core)], g_in.at[0], g_ss.at[0], g_rs.at[0], space=partner(strides[0]))
        if i < nb:
            return copy(g_out.at[i], g_in.at[i], g_ss.at[i], g_rs.at[i], space=partner(strides[i]))
        at = half_at(core)
        return copy(g_fin.at[at], g_fin.at[at], g_ss.at[i], g_rs.at[i], space=partner(strides[0]))

    def g_step(i):
        own = gr[half_at(core), :] if i == 1 else g_out[i - 1]
        g_copy(i - 1).wait_recv()
        total = own + g_in[i - 1]
        if i < nb:
            g_out[i] = total
        else:
            g_fin[half_at(core), :] = total
        g_copy(i).start()

    gr[...] = dot(skt[...], sk[...])
    g_copy(0).start()

    width = 2 * rank if cols % (2 * rank) == 0 else rank
    blocks = cols // width
    cr[:, cols:] = jnp.zeros((rank, sw), F32)
    cr[:, cols : cols + sc] = dot(skt[...], win_s[...])
    for i in range(nb):

        @pl.loop(blocks * i // nb, blocks * (i + 1) // nb)
        def _(b):
            at = pl.ds(pl.multiple_of(b * width, width), width)
            cr[:, at] = dot(skt[...], win[:, at])

        if i + 1 < nb:
            g_step(i + 1)

    def c_copy(i):
        if i < nb:
            return copy(c_out.at[i], c_in.at[i], c_ss.at[i], c_rs.at[i], space=partner(strides[i]))
        at = half_at(core)
        return copy(c_fin.at[at], c_fin.at[at], c_ss.at[i], c_rs.at[i], space=partner(strides[0]))

    c_out[0] = cr[half_at(1 - core), :].astype(BF16)
    c_copy(0).start()

    def c_step(i):
        c_copy(i - 1).wait_recv()
        own = cr[half_at(core), :] if i == 1 else c_out[i - 1].astype(F32)
        total = (own + c_in[i - 1].astype(F32)).astype(BF16)
        if i < nb:
            c_out[i] = total
        else:
            c_fin[half_at(core), :] = total
        c_copy(i).start()

    def sl_copy(d):
        return copy(
            c_fin.at[:, pl.ds(cols, sw)], sl_in.at[d], sl_ss.at[d], sl_rs.at[d], slot=lax.rem(z + d, n)
        )

    def sl_start():
        c_copy(nb).wait_recv()
        for d in range(1, n):
            sl_copy(d).start()

    g_step(nb)
    c_step(1)
    g_copy(nb).wait_recv()

    steps = [functools.partial(c_step, i) for i in range(2, nb + 1)] + [sl_start]
    cut = (len(steps) + 1) // 2
    scale = 1.0 / total_rows
    t_ref[...] = g_fin[:half, :half] * scale
    inv1 = inverse_lower(t_ref, half, steps[:cut])
    low = dot_full(g_fin[half:, :half] * scale, inv1, ((1,), (1,)))
    t_ref[...] = g_fin[half:, half:] * scale - dot_full(low, low, ((1,), (1,)))
    inv2 = inverse_lower(t_ref, half, steps[cut:])
    inv_ref[:half, :half] = inv1
    inv_ref[:half, half:] = jnp.zeros((half, half), F32)
    inv_ref[half:, :half] = -dot_full(inv2, dot_full(low, inv1))
    inv_ref[half:, half:] = inv2

    hi, lo = split(inv_ref[...])

    @pl.loop(0, n)
    def _(c):
        at = pl.ds(pl.multiple_of(c * chunk, chunk), chunk)
        s = sk[at, :]
        basis_o[at, :] = (dot(s, hi, ((1,), (1,))) + dot(s, lo, ((1,), (1,)))).astype(BF16)

    for d in range(1, n):
        sl_copy(d).wait_recv()
    norm = 1.0 / (total_rows ** 0.5)

    @pl.loop(0, blocks)
    def _(b):
        at = pl.ds(pl.multiple_of(b * width, width), width)
        x = c_fin[:, at].astype(F32)
        for d in range(n):
            src = lax.rem(z + n - d, n)
            p = place[pl.ds(pl.multiple_of(src * sc, sc), sc), at]
            own = c_fin[:, cols : cols + sc] if d == 0 else sl_in[d, :, :sc]
            x += dot(own, p)
        x = x.astype(BF16)
        coef_o[:, at] = (dot(hi, x) + dot(lo, x)) * norm

    for d in range(1, n):
        tm_copy(d).wait_send()
        sl_copy(d).wait_send()
        for h in range(SUB):
            for way in (0, 1):
                c = z + d * (1 - 2 * way)

                @pl.when((c >= 0) & (c < n))
                def _():
                    rs_copy(way, c, h).wait_send()

    for d in range(n):
        for h in range(SUB):
            for way in (0, 1):
                c = z - d * (1 - 2 * way)

                @pl.when((c >= 0) & (c < n) & has[1 - way])
                def _():
                    ag_copy(way, c, h).wait_send()

    for i in range(nb + 1):
        g_copy(i).wait_send()
        c_copy(i).wait_send()


def local(n, nsp, vals, scales, slab, slab_sc, test, owner, offset):
    rows, cols = vals.shape
    rank = test.shape[1]
    sc = slab.shape[1]
    sw = -(-sc // 128) * 128
    nb = nsp.bit_length() - 1
    half = rank // 2
    vmem = pl.BlockSpec(memory_space=pltpu.VMEM)
    smem = pl.BlockSpec(memory_space=pltpu.SMEM)
    dma = pltpu.SemaphoreType.DMA
    flops = 2 * rank * (2 * rows * cols + 3 * rank * rows + 2 * rank * cols)
    return pl.pallas_call(
        functools.partial(kernel, n, nsp),
        out_shape=(
            jax.ShapeDtypeStruct((rows, rank), BF16),
            jax.ShapeDtypeStruct((rank, cols), F32),
        ),
        in_specs=[vmem] * 5 + [smem] * 2,
        out_specs=(vmem, vmem),
        scratch_shapes=[
            pltpu.VMEM((rows, cols), BF16),
            pltpu.VMEM((rows, sc), BF16),
            pltpu.VMEM(scales.shape, F32),
            pltpu.VMEM((n * sc, cols), BF16),
            pltpu.VMEM((n, sc, rank), BF16),
            pltpu.VMEM((n, sc, rank), BF16),
            pltpu.VMEM((rows, rank), F32),
            pltpu.VMEM((2, rows, rank), BF16),
            pltpu.VMEM((2, rows, rank), BF16),
            pltpu.VMEM((rows, rank), BF16),
            pltpu.VMEM((rank, rows), BF16),
            pltpu.VMEM((rank, rank), F32),
            pltpu.VMEM((nb, half, rank), F32),
            pltpu.VMEM((nb, half, rank), F32),
            pltpu.VMEM((rank, rank), F32),
            pltpu.VMEM((rank, cols + sw), F32),
            pltpu.VMEM((nb, half, cols + sw), BF16),
            pltpu.VMEM((nb, half, cols + sw), BF16),
            pltpu.VMEM((rank, cols + sw), BF16),
            pltpu.VMEM((n, rank, sw), BF16),
            pltpu.VMEM((half, half), F32),
            pltpu.VMEM((rank, rank), F32),
            dma((n,)), dma((n,)),
            dma((n, SUB)), dma((n, SUB)), dma((n, SUB)), dma((n, SUB)),
            dma((n, SUB)), dma((n, SUB)), dma((n, SUB)), dma((n, SUB)),
            dma((nb + 1,)), dma((nb + 1,)), dma((nb + 1,)), dma((nb + 1,)),
            dma((n,)), dma((n,)),
        ],
        compiler_params=pltpu.CompilerParams(
            collective_id=0, has_side_effects=True, vmem_limit_bytes=60 * 2 ** 20
        ),
        cost_estimate=pl.CostEstimate(
            flops=flops, bytes_accessed=2 * rows * cols + 4 * rank * cols, transcendentals=0
        ),
    )(vals, scales, slab, slab_sc, test, owner, offset)


def solution(mesh):
    return jax.shard_map(
        functools.partial(local, mesh.shape["slot"], mesh.shape["space"]),
        mesh=mesh,
        in_specs=(
            P("space", "slot"),
            P("space", "slot"),
            P("space", "slot"),
            P("space", "slot"),
            P("slot", None),
            P(),
            P(),
        ),
        out_specs=(P("space", None), P(None, "slot")),
        check_vma=False,
    )
```

time: 360 us -> 107 us (0.30)
  waiting for transfers between devices: 182 us -> 0 us
  Pallas kernels: 0 us -> 101 us
  other arithmetic: 74.2 us -> 0 us
  matrix products: 35.9 us -> 0 us
  local copies, waits for them, and re-layouts: 37 us -> 3.73 us
  between operations: 16 us -> 1.3 us
  blocking collectives: 13.6 us -> 0 us
    psum x2 -> x0, waiting for transfers between devices: 148 us -> none  [the longest x1 85.5 us: local(): lax.psum(jnp.dot(window, test_matrix, preferred_element_type=jnp.float32)...]
    pallas_call x0 -> x1, Pallas kernels: none -> 101 us  [local(): pl.pallas_call(functools.partial(kernel, n, nsp), out_shape=(jax.ShapeDty...]
    another operation x9 -> x0, other arithmetic: 58.6 us -> none  [the longest x6 36.5 us: factor(): lower_factor = jnp.linalg.cholesky(gram_matrix / cell_count)]
    all_gather x1 -> x0, waiting for transfers between devices: 34.2 us -> none  [local(): lax.all_gather(slab_values, 'slot', axis=1, tiled=True)]
    dot_general x5 -> x0, matrix products: 30.6 us -> none  [the longest x1 11.8 us: inner_rows(): lax.dot_general(left, right, (((0,), (0,)), ((), ())), precision=lax.Prec...]
    dynamic_update_slice x2 -> x0, local copies, waits for them, and re-layouts: 21.6 us -> none  [the longest x1 21.1 us: local(): lax.dynamic_update_slice_in_dim(window_values, jnp.where(is_owner, slab_w...]
    all_gather x1 -> x0, blocking collectives: 13.6 us -> none  [local(): lax.all_gather(slab_scales, 'slot', axis=1, tiled=True)]
    convert_element_type x2 -> x0, other arithmetic: 9.74 us -> none  [the longest x1 9.73 us: expand(): return scaled.reshape(row_count, col_count).astype(jnp.bfloat16)]
  transfers between devices with their start and end apart: 3 -> 0, of which waited for: 3 -> 0; matrix products, arithmetic and copies ran while one was open for 0% -> 0% of each run, Pallas kernels for 0% -> 0%
where the time goes in v1:
time: 107 us; the launch traced here: 106 us
  Pallas kernels  101 us (94%)
  local copies, waits for them, and re-layouts  3.73 us (3%)
  between operations  1.3 us (1%)
    pallas_call x1, Pallas kernels, local(): pl.pallas_call(functools.partial(kernel, n, nsp), out_shape=(jax.ShapeDty...  101 us
    unnamed x4, local copies, waits for them, and re-layouts  3.73 us

profile of v1, /device:TPU:0, one launch (start us, length us, event | category | flops | bytes accessed | tf_op | source)
XLA Modules:
  0.0 106.4 jit_solution(10993347886535441924)
XLA Ops:
  1.3 101.4 %shard_map.86 = (bf16[2048,256]{1,0:T(8,128)(2,1)}, f32[256,2048]{1,0:T(8,128)}) custom-call(bf16[2048,2048]{1,0:T(8,128)(2,1)} %vals.1, bf16[16,2048]{1,0:T(8,128)(2,1)} %scales.1, bf16[2048,128]{1,0:T(8,128)(2,1)} %slab.1, bf16[16,128]{1,0:T(8,128)(2,1)} %slab_sc.1, bf16[2048,256]{1,0:T(8,128)(2,1)} %test.1, s32[4]{0:T(128)} %owner.1, s32[1]{0:T(128)S(6)} %copy.11.offset), custom_call_target="tpu_custom_call" | custom-call | flops 5637144576 | bytes 10485760 | tf_op jit(solution)/shard_map/pallas_call | solution.py:374
  102.7 0.0 copy-start
  102.7 2.4 %copy.12 = bf16[2048,256]{1,0:T(8,128)(2,1)} copy(bf16[2048,256]{1,0:T(8,128)(2,1)} %get-tuple-element.4) | data formatting | bytes 2097152
  105.1 0.0 copy-done
  105.1 1.3 %copy.13 = f32[256,2048]{1,0:T(8,128)} copy(f32[256,2048]{1,0:T(8,128)S(1)} %copy-done) | data formatting | bytes 4194304
Async XLA Ops:
  102.7 2.4 %copy-start = (f32[256,2048]{1,0:T(8,128)S(1)}, f32[256,2048]{1,0:T(8,128)}, u32[]{:S(2)}) copy-start(f32[256,2048]{1,0:T(8,128)} %get-tuple-element.5) | copy-start | bytes 6291460

commit v2 on v1

--- a/solution.py
+++ b/solution.py
@@ -35,19 +35,27 @@
     lane1 = lax.broadcasted_iota(jnp.int32, (1, size), 1)
 
     def round_of(g, _):
-        t = t_ref[...]
-        tile = t_ref[pl.ds(pl.multiple_of(g * 8, 8), 8), :]
+        rest = t_ref[8:, :]
+        tile = t_ref[:8, :]
+        cols = [jnp.broadcast_to(tile[:, j : j + 1], (8, size)) for j in range(8)]
+        inv8 = jnp.zeros((8, size), F32)
         for s in range(8):
-            below = row > g * 8 + s
-            below8 = sub8 > s
-            r = tile[s : s + 1, :]
-            inv = 1.0 / tile[s : s + 1, s : s + 1]
-            r = jnp.where(lane1 == s, 1.0, r) * inv
-            col8 = jnp.where(below8, tile[:, s : s + 1], 0.0)
-            tile = jnp.where(below8 & (lane8 == s), 0.0, tile) - col8 * r
-            col = jnp.where(below, t[:, s : s + 1], 0.0)
-            t = jnp.where(below & (lane == s), 0.0, t) - col * r
-        t_ref[...] = pltpu.roll(t, size - 8, 1)
+            inv = 1.0 / cols[s][s : s + 1, :]
+            inv8 = jnp.where(sub8 == s, inv, inv8)
+            m = jnp.where(sub8 > s, cols[s] * inv, 0.0)
+            r = jnp.where(lane1 == s, 1.0, tile[s : s + 1, :])
+            for j in range(s + 1, 8):
+                cols[j] = cols[j] - m * cols[j][s : s + 1, :]
+            tile = jnp.where((sub8 > s) & (lane8 == s), 0.0, tile) - m * r
+        left = size - 8 * g
+        mult = jnp.where((lane8 >= 8) & (lane8 < left), tile * inv8, 0.0)
+        unit = jnp.where(lane8 < sub8, tile, jnp.where(lane8 == sub8, 1.0, 0.0))
+        rows = jnp.where(lane8 < 8, unit, tile)
+        change = dot_full(mult, rows, ((0,), (0,)))
+        open_rows = (row[8:] < left) & (lane[8:] < 8)
+        rest = jnp.where(open_rows, 0.0, rest) - change[8:]
+        t_ref[: size - 8, :] = pltpu.roll(rest, size - 8, 1)
+        t_ref[size - 8 :, :] = pltpu.roll(tile, size - 8, 1)
         return 0
 
     rounds = size // 8

time: 107 us -> 102 us (0.953)
  Pallas kernels: 101 us -> 96.8 us
    pallas_call x1, Pallas kernels: 101 us -> 96.8 us  [local(): pl.pallas_call(functools.partial(kernel, n, nsp), out_shape=(jax.ShapeDty...]
where the time goes in v2:
time: 102 us
  Pallas kernels  96.8 us (95%)
  local copies, waits for them, and re-layouts  3.73 us (4%)
  between operations  1.3 us (1%)
    pallas_call x1, Pallas kernels, local(): pl.pallas_call(functools.partial(kernel, n, nsp), out_shape=(jax.ShapeDty...  96.8 us
    unnamed x4, local copies, waits for them, and re-layouts  3.73 us

profile of v2, /device:TPU:0, one launch (start us, length us, event | category | flops | bytes accessed | tf_op | source)
XLA Modules:
  0.0 101.8 jit_solution(9127287351889208868)
XLA Ops:
  1.3 96.8 %shard_map.86 = (bf16[2048,256]{1,0:T(8,128)(2,1)}, f32[256,2048]{1,0:T(8,128)}) custom-call(bf16[2048,2048]{1,0:T(8,128)(2,1)} %vals.1, bf16[16,2048]{1,0:T(8,128)(2,1)} %scales.1, bf16[2048,128]{1,0:T(8,128)(2,1)} %slab.1, bf16[16,128]{1,0:T(8,128)(2,1)} %slab_sc.1, bf16[2048,256]{1,0:T(8,128)(2,1)} %test.1, s32[4]{0:T(128)} %owner.1, s32[1]{0:T(128)S(6)} %copy.11.offset), custom_call_target="tpu_custom_call" | custom-call | flops 5637144576 | bytes 10485760 | tf_op jit(solution)/shard_map/pallas_call | solution.py:382
  98.1 0.0 copy-start
  98.1 2.4 %copy.12 = bf16[2048,256]{1,0:T(8,128)(2,1)} copy(bf16[2048,256]{1,0:T(8,128)(2,1)} %get-tuple-element.4) | data formatting | bytes 2097152
  100.5 0.0 copy-done
  100.5 1.3 %copy.13 = f32[256,2048]{1,0:T(8,128)} copy(f32[256,2048]{1,0:T(8,128)S(1)} %copy-done) | data formatting | bytes 4194304
Async XLA Ops:
  98.1 2.4 %copy-start = (f32[256,2048]{1,0:T(8,128)S(1)}, f32[256,2048]{1,0:T(8,128)}, u32[]{:S(2)}) copy-start(f32[256,2048]{1,0:T(8,128)} %get-tuple-element.5) | copy-start | bytes 6291460

commit v3 on v2

--- a/solution.py
+++ b/solution.py
@@ -9,7 +9,8 @@
 
 MESH = pl.DeviceIdType.MESH
 F32, BF16 = jnp.float32, jnp.bfloat16
-SUB = 2
+SUB = 4
+PIECES = 4
 
 
 def dot(a, b, contract=((1,), (0,))):
@@ -58,13 +59,13 @@
         t_ref[size - 8 :, :] = pltpu.roll(tile, size - 8, 1)
         return 0
 
-    rounds = size // 8
-    parts = len(between) + 1
-    edges = [rounds * i // parts for i in range(parts + 1)]
-    for i in range(parts):
-        lax.fori_loop(edges[i], edges[i + 1], round_of, 0)
-        if i < len(between):
-            between[i]()
+    done, rounds = 0, size // 8
+    for at, action in between:
+        at = min(int(at * rounds), rounds)
+        lax.fori_loop(done, at, round_of, 0)
+        action()
+        done = at
+    lax.fori_loop(done, rounds, round_of, 0)
     t = t_ref[...]
     pivot = jnp.sum(jnp.where(row == lane, t, 0.0), axis=1, keepdims=True)
     unit = jnp.where(row > lane, t, jnp.where(row == lane, 1.0, 0.0))
@@ -74,11 +75,11 @@
 def kernel(
     n, nsp,
     vals, scales, slab, slab_sc, test, owner, offset,
-    basis_o, coef_o,
-    win, win_s, msc, place, tm_out, tm_in, part, rs_out, rs_in, sk, skt,
-    gr, g_out, g_in, g_fin, cr, c_out, c_in, c_fin, sl_in, t_ref, inv_ref,
+    sk_o, x_o, inv_ref,
+    vbuf, win, win_s, msc, place, tm_out, tm_in, part, rs_out, rs_in, sk, skt,
+    gr, g_out, g_in, g_fin, cr, c_out, c_in, c_fin, sl_in, t_ref, gpart,
     tm_ss, tm_rs, rr_ss, rr_rs, rl_ss, rl_rs, ar_ss, ar_rs, al_ss, al_rs,
-    g_ss, g_rs, c_ss, c_rs, sl_ss, sl_rs,
+    g_ss, g_rs, c_ss, c_rs, sl_ss, sl_rs, v_sem, o_sem,
 ):
     z = lax.axis_index("slot")
     me = lax.axis_index("space")
@@ -109,6 +110,13 @@
             device_id_type=MESH,
         )
 
+    def load(c):
+        at = pl.ds(pl.multiple_of(c * chunk, chunk), chunk)
+        return pltpu.make_async_copy(vals.at[at], vbuf.at[at], v_sem.at[c])
+
+    for c in range(n):
+        load(c).start()
+
     barrier = pltpu.get_barrier_semaphore()
     for d in range(1, n):
         pl.semaphore_signal(
@@ -149,12 +157,17 @@
             slab[b * block : (b + 1) * block, :].astype(F32) * ssc[b : b + 1, :]
         ).astype(BF16)
 
-    @pl.loop(0, rows // block)
-    def _(b):
-        at = pl.ds(pl.multiple_of(b * block, block), block)
-        w = (vals[at, :].astype(F32) * msc[pl.ds(b, 1), :]).astype(BF16)
-        win[at, :] = w
-        part[at, :] = dot(w, test[...])
+    @pl.loop(0, n)
+    def _(c):
+        load(c).wait()
+
+        @pl.loop(0, chunk // block)
+        def _(i):
+            b = c * (chunk // block) + i
+            at = pl.ds(pl.multiple_of(b * block, block), block)
+            w = (vbuf[at, :].astype(F32) * msc[pl.ds(b, 1), :]).astype(BF16)
+            win[at, :] = w
+            part[at, :] = dot(w, test[...])
 
     rows_new = tm_out[z].astype(F32)
     for d in range(1, n):
@@ -162,8 +175,7 @@
         rows_new += tm_in[d].astype(F32)
     rows_new = rows_new.astype(BF16)
 
-    @pl.loop(0, n)
-    def _(c):
+    def add_new(c):
         at = pl.ds(pl.multiple_of(c * chunk, chunk), chunk)
         part[at, :] += dot(win_s[at, :], rows_new)
 
@@ -180,6 +192,13 @@
 
     has = (z > 0, z < n - 1)
     for d in range(n - 1, 0, -1):
+        for way in (0, 1):
+            c = z + d * (1 - 2 * way)
+
+            @pl.when((c >= 0) & (c < n))
+            def _():
+                add_new(c)
+
         for h in range(SUB):
             for way in (0, 1):
                 c = z + d * (1 - 2 * way)
@@ -196,6 +215,8 @@
                     rs_out[way, at, :] = part[at, :].astype(BF16)
                     rs_copy(way, c, h).start()
 
+    add_new(z)
+
     def ag_copy(way, c, h):
         ss, rs = ((ar_ss, ar_rs), (al_ss, al_rs))[way]
         at = span(c, h)
@@ -217,7 +238,37 @@
             def _():
                 ag_copy(way, z, h).start()
 
+    width = 2 * rank if cols % (2 * rank) == 0 else rank
+    blocks = cols // width
+    cr[...] = jnp.zeros(cr.shape, F32)
+
+    def gram_of(c):
+        at = pl.ds(pl.multiple_of(c * chunk, chunk), chunk)
+        s = sk[at, :]
+        t = s.astype(F32).T.astype(BF16)
+        skt[:, at] = t
+        gpart[c] = dot(t, s)
+
+    def cross_of(c):
+        at = pl.ds(pl.multiple_of(c * chunk, chunk), chunk)
+        t = skt[:, at]
+        cr[:, cols : cols + sc] += dot(t, win_s[at, :])
+
+        @pl.loop(0, blocks)
+        def _(b):
+            to = pl.ds(pl.multiple_of(b * width, width), width)
+            cr[:, to] += dot(t, win[at, to])
+
+    def at_distance(d, action):
+        for c in (z - d, z + d)[: 2 if d else 1]:
+
+            @pl.when((c >= 0) & (c < n))
+            def _():
+                action(c)
+
+    gram_of(z)
     for d in range(1, n):
+        at_distance(d - 1, cross_of)
         for h in range(SUB):
             for way in (0, 1):
                 c = z - d * (1 - 2 * way)
@@ -230,10 +281,10 @@
                     def _():
                         ag_copy(way, c, h).start()
 
-    @pl.loop(0, n)
-    def _(c):
-        at = pl.ds(pl.multiple_of(c * chunk, chunk), chunk)
-        skt[:, at] = sk[at, :].astype(F32).T.astype(BF16)
+        at_distance(d, gram_of)
+
+    out_sk = pltpu.make_async_copy(sk, sk_o, o_sem.at[0])
+    out_sk.start()
 
     def half_at(c):
         return pl.ds(pl.multiple_of(c * half, half), half)
@@ -256,22 +307,14 @@
             g_fin[half_at(core), :] = total
         g_copy(i).start()
 
-    gr[...] = dot(skt[...], sk[...])
+    total = gpart[0]
+    for c in range(1, n):
+        total += gpart[c]
+    gr[...] = total
     g_copy(0).start()
-
-    width = 2 * rank if cols % (2 * rank) == 0 else rank
-    blocks = cols // width
-    cr[:, cols:] = jnp.zeros((rank, sw), F32)
-    cr[:, cols : cols + sc] = dot(skt[...], win_s[...])
-    for i in range(nb):
-
-        @pl.loop(blocks * i // nb, blocks * (i + 1) // nb)
-        def _(b):
-            at = pl.ds(pl.multiple_of(b * width, width), width)
-            cr[:, at] = dot(skt[...], win[:, at])
-
-        if i + 1 < nb:
-            g_step(i + 1)
+    at_distance(n - 1, cross_of)
+    for i in range(1, nb):
+        g_step(i)
 
     def c_copy(i):
         if i < nb:
@@ -307,29 +350,22 @@
     g_copy(nb).wait_recv()
 
     steps = [functools.partial(c_step, i) for i in range(2, nb + 1)] + [sl_start]
-    cut = (len(steps) + 1) // 2
+    spots = [(0.5 + i * 1.0 / len(steps), f) for i, f in enumerate(steps)]
+    early = [(at, f) for at, f in spots if at < 1]
+    late = [(at - 1, f) for at, f in spots if at >= 1]
     scale = 1.0 / total_rows
     t_ref[...] = g_fin[:half, :half] * scale
-    inv1 = inverse_lower(t_ref, half, steps[:cut])
+    inv1 = inverse_lower(t_ref, half, early)
     low = dot_full(g_fin[half:, :half] * scale, inv1, ((1,), (1,)))
     t_ref[...] = g_fin[half:, half:] * scale - dot_full(low, low, ((1,), (1,)))
-    inv2 = inverse_lower(t_ref, half, steps[cut:])
+    inv2 = inverse_lower(t_ref, half, late)
     inv_ref[:half, :half] = inv1
     inv_ref[:half, half:] = jnp.zeros((half, half), F32)
     inv_ref[half:, :half] = -dot_full(inv2, dot_full(low, inv1))
     inv_ref[half:, half:] = inv2
 
-    hi, lo = split(inv_ref[...])
-
-    @pl.loop(0, n)
-    def _(c):
-        at = pl.ds(pl.multiple_of(c * chunk, chunk), chunk)
-        s = sk[at, :]
-        basis_o[at, :] = (dot(s, hi, ((1,), (1,))) + dot(s, lo, ((1,), (1,)))).astype(BF16)
-
     for d in range(1, n):
         sl_copy(d).wait_recv()
-    norm = 1.0 / (total_rows ** 0.5)
 
     @pl.loop(0, blocks)
     def _(b):
@@ -340,8 +376,7 @@
             p = place[pl.ds(pl.multiple_of(src * sc, sc), sc), at]
             own = c_fin[:, cols : cols + sc] if d == 0 else sl_in[d, :, :sc]
             x += dot(own, p)
-        x = x.astype(BF16)
-        coef_o[:, at] = (dot(hi, x) + dot(lo, x)) * norm
+        x_o[:, at] = x.astype(BF16)
 
     for d in range(1, n):
         tm_copy(d).wait_send()
@@ -366,6 +401,15 @@
     for i in range(nb + 1):
         g_copy(i).wait_send()
         c_copy(i).wait_send()
+    out_sk.wait()
+
+
+def apply(total_rows, sk, x, inv, basis_o, coef_o):
+    hi, lo = split(inv[...])
+    s = sk[...]
+    basis_o[...] = (dot(s, hi, ((1,), (1,))) + dot(s, lo, ((1,), (1,)))).astype(BF16)
+    v = x[...]
+    coef_o[...] = (dot(hi, v) + dot(lo, v)) * (1.0 / total_rows ** 0.5)
 
 
 def local(n, nsp, vals, scales, slab, slab_sc, test, owner, offset):
@@ -379,15 +423,17 @@
     smem = pl.BlockSpec(memory_space=pltpu.SMEM)
     dma = pltpu.SemaphoreType.DMA
     flops = 2 * rank * (2 * rows * cols + 3 * rank * rows + 2 * rank * cols)
-    return pl.pallas_call(
+    sk, x, inv = pl.pallas_call(
         functools.partial(kernel, n, nsp),
         out_shape=(
             jax.ShapeDtypeStruct((rows, rank), BF16),
-            jax.ShapeDtypeStruct((rank, cols), F32),
-        ),
-        in_specs=[vmem] * 5 + [smem] * 2,
-        out_specs=(vmem, vmem),
+            jax.ShapeDtypeStruct((rank, cols), BF16),
+            jax.ShapeDtypeStruct((rank, rank), F32),
+        ),
+        in_specs=[pl.BlockSpec(memory_space=pl.ANY)] + [vmem] * 4 + [smem] * 2,
+        out_specs=(pl.BlockSpec(memory_space=pl.ANY), vmem, vmem),
         scratch_shapes=[
+            pltpu.VMEM((rows, cols), BF16),
             pltpu.VMEM((rows, cols), BF16),
             pltpu.VMEM((rows, sc), BF16),
             pltpu.VMEM(scales.shape, F32),
@@ -409,12 +455,12 @@
             pltpu.VMEM((rank, cols + sw), BF16),
             pltpu.VMEM((n, rank, sw), BF16),
             pltpu.VMEM((half, half), F32),
-            pltpu.VMEM((rank, rank), F32),
+            pltpu.VMEM((n, rank, rank), F32),
             dma((n,)), dma((n,)),
             dma((n, SUB)), dma((n, SUB)), dma((n, SUB)), dma((n, SUB)),
             dma((n, SUB)), dma((n, SUB)), dma((n, SUB)), dma((n, SUB)),
             dma((nb + 1,)), dma((nb + 1,)), dma((nb + 1,)), dma((nb + 1,)),
-            dma((n,)), dma((n,)),
+            dma((n,)), dma((n,)), dma((n,)), dma((1,)),
         ],
         compiler_params=pltpu.CompilerParams(
             collective_id=0, has_side_effects=True, vmem_limit_bytes=60 * 2 ** 20
@@ -423,6 +469,27 @@
             flops=flops, bytes_accessed=2 * rows * cols + 4 * rank * cols, transcendentals=0
         ),
     )(vals, scales, slab, slab_sc, test, owner, offset)
+    return pl.pallas_call(
+        functools.partial(apply, rows * nsp),
+        out_shape=(
+            jax.ShapeDtypeStruct((rows, rank), BF16),
+            jax.ShapeDtypeStruct((rank, cols), F32),
+        ),
+        grid=(PIECES,),
+        in_specs=[
+            pl.BlockSpec((rows // PIECES, rank), lambda i: (i, 0)),
+            pl.BlockSpec((rank, cols // PIECES), lambda i: (0, i)),
+            pl.BlockSpec((rank, rank), lambda i: (0, 0)),
+        ],
+        out_specs=(
+            pl.BlockSpec((rows // PIECES, rank), lambda i: (i, 0)),
+            pl.BlockSpec((rank, cols // PIECES), lambda i: (0, i)),
+        ),
+        cost_estimate=pl.CostEstimate(
+            flops=4 * rank * rank * (rows + cols), bytes_accessed=4 * rank * (rows + cols),
+            transcendentals=0,
+        ),
+    )(sk, x, inv)
 
 
 def solution(mesh):

time: 102 us -> 95 us (0.931)
  local copies, waits for them, and re-layouts: 3.73 us -> 0 us
  Pallas kernels: 96.8 us -> 93.5 us
    pallas_call x1, Pallas kernels: 96.8 us -> 88.6 us  [local(): pl.pallas_call(functools.partial(kernel, n, nsp), out_shape=(jax.ShapeDty...]
    pallas_call x0 -> x1, Pallas kernels: none -> 4.88 us  [local(): pl.pallas_call(functools.partial(apply, rows * nsp), out_shape=(jax.Shape...]
    unnamed x4 -> x0, local copies, waits for them, and re-layouts: 3.73 us -> none
where the time goes in v3:
time: 95 us; the launch traced here: 94.8 us
  Pallas kernels  93.5 us (98%)
  between operations  1.29 us (1%)
    pallas_call x1, Pallas kernels, local(): pl.pallas_call(functools.partial(kernel, n, nsp), out_shape=(jax.ShapeDty...  88.6 us
    pallas_call x1, Pallas kernels, local(): pl.pallas_call(functools.partial(apply, rows * nsp), out_shape=(jax.Shape...  4.88 us

profile of v3, /device:TPU:0, one launch (start us, length us, event | category | flops | bytes accessed | tf_op | source)
XLA Modules:
  0.0 94.8 jit_solution(6943906939025005635)
XLA Ops:
  1.3 88.6 %shard_map.86 = (bf16[2048,256]{1,0:T(8,128)(2,1)}, bf16[256,2048]{1,0:T(8,128)(2,1)}, f32[256,256]{1,0:T(8,128)}) custom-call(bf16[2048,2048]{1,0:T(8,128)(2,1)} %vals.1, bf16[16,2048]{1,0:T(8,128)(2,1)} %scales.1, bf16[2048,128]{1,0:T(8,128)(2,1)} %slab.1, bf16[16,128]{1,0:T(8,128)(2,1)} %slab_sc.1, bf16[2048,256]{1,0:T(8,128)(2,1)} %test.1, s32[4]{0:T(128)} %owner.1, ...), custom_call_target="tpu_custom_call" | custom-call | flops 5637144576 | bytes 10485760 | tf_op jit(solution)/shard_map/pallas_call | solution.py:426
  89.9 4.9 %shard_map.87 = (bf16[2048,256]{1,0:T(8,128)(2,1)}, f32[256,2048]{1,0:T(8,128)}) custom-call(bf16[2048,256]{1,0:T(8,128)(2,1)} %get-tuple-element.5.sk, bf16[256,2048]{1,0:T(8,128)(2,1)} %get-tuple-element.6.x, f32[256,256]{1,0:T(8,128)} %get-tuple-element.7.inv), custom_call_target="tpu_custom_call" | custom-call | flops 1073741824 | bytes 4194304 | tf_op jit(solution)/shard_map/pallas_call | solution.py:472

commit v4 on v3

--- a/solution.py
+++ b/solution.py
@@ -11,6 +11,7 @@
 F32, BF16 = jnp.float32, jnp.bfloat16
 SUB = 4
 PIECES = 4
+WIDE = 16
 
 
 def dot(a, b, contract=((1,), (0,))):
@@ -31,35 +32,35 @@
 def inverse_lower(t_ref, size, between):
     row = lax.broadcasted_iota(jnp.int32, (size, size), 0)
     lane = lax.broadcasted_iota(jnp.int32, (size, size), 1)
-    sub8 = lax.broadcasted_iota(jnp.int32, (8, size), 0)
-    lane8 = lax.broadcasted_iota(jnp.int32, (8, size), 1)
+    sub = lax.broadcasted_iota(jnp.int32, (WIDE, size), 0)
+    lane_t = lax.broadcasted_iota(jnp.int32, (WIDE, size), 1)
     lane1 = lax.broadcasted_iota(jnp.int32, (1, size), 1)
 
     def round_of(g, _):
-        rest = t_ref[8:, :]
-        tile = t_ref[:8, :]
-        cols = [jnp.broadcast_to(tile[:, j : j + 1], (8, size)) for j in range(8)]
-        inv8 = jnp.zeros((8, size), F32)
-        for s in range(8):
+        rest = t_ref[WIDE:, :]
+        tile = t_ref[:WIDE, :]
+        cols = [jnp.broadcast_to(tile[:, j : j + 1], (WIDE, size)) for j in range(WIDE)]
+        inv_t = jnp.zeros((WIDE, size), F32)
+        for s in range(WIDE):
             inv = 1.0 / cols[s][s : s + 1, :]
-            inv8 = jnp.where(sub8 == s, inv, inv8)
-            m = jnp.where(sub8 > s, cols[s] * inv, 0.0)
+            inv_t = jnp.where(sub == s, inv, inv_t)
+            m = jnp.where(sub > s, cols[s], 0.0) * inv
             r = jnp.where(lane1 == s, 1.0, tile[s : s + 1, :])
-            for j in range(s + 1, 8):
+            for j in range(s + 1, WIDE):
                 cols[j] = cols[j] - m * cols[j][s : s + 1, :]
-            tile = jnp.where((sub8 > s) & (lane8 == s), 0.0, tile) - m * r
-        left = size - 8 * g
-        mult = jnp.where((lane8 >= 8) & (lane8 < left), tile * inv8, 0.0)
-        unit = jnp.where(lane8 < sub8, tile, jnp.where(lane8 == sub8, 1.0, 0.0))
-        rows = jnp.where(lane8 < 8, unit, tile)
+            tile = jnp.where((sub > s) & (lane_t == s), 0.0, tile) - m * r
+        left = size - WIDE * g
+        mult = jnp.where((lane_t >= WIDE) & (lane_t < left), tile * inv_t, 0.0)
+        unit = jnp.where(lane_t < sub, tile, jnp.where(lane_t == sub, 1.0, 0.0))
+        rows = jnp.where(lane_t < WIDE, unit, tile)
         change = dot_full(mult, rows, ((0,), (0,)))
-        open_rows = (row[8:] < left) & (lane[8:] < 8)
-        rest = jnp.where(open_rows, 0.0, rest) - change[8:]
-        t_ref[: size - 8, :] = pltpu.roll(rest, size - 8, 1)
-        t_ref[size - 8 :, :] = pltpu.roll(tile, size - 8, 1)
+        open_rows = (row[WIDE:] < left) & (lane[WIDE:] < WIDE)
+        rest = jnp.where(open_rows, 0.0, rest) - change[WIDE:]
+        t_ref[: size - WIDE, :] = pltpu.roll(rest, size - WIDE, 1)
+        t_ref[size - WIDE :, :] = pltpu.roll(tile, size - WIDE, 1)
         return 0
 
-    done, rounds = 0, size // 8
+    done, rounds = 0, size // WIDE
     for at, action in between:
         at = min(int(at * rounds), rounds)
         lax.fori_loop(done, at, round_of, 0)
@@ -313,8 +314,6 @@
     gr[...] = total
     g_copy(0).start()
     at_distance(n - 1, cross_of)
-    for i in range(1, nb):
-        g_step(i)
 
     def c_copy(i):
         if i < nb:
@@ -322,8 +321,11 @@
         at = half_at(core)
         return copy(c_fin.at[at], c_fin.at[at], c_ss.at[i], c_rs.at[i], space=partner(strides[0]))
 
+    g_step(1)
     c_out[0] = cr[half_at(1 - core), :].astype(BF16)
     c_copy(0).start()
+    for i in range(2, nb):
+        g_step(i)
 
     def c_step(i):
         c_copy(i - 1).wait_recv()
@@ -345,8 +347,8 @@
         for d in range(1, n):
             sl_copy(d).start()
 
+    c_step(1)
     g_step(nb)
-    c_step(1)
     g_copy(nb).wait_recv()
 
     steps = [functools.partial(c_step, i) for i in range(2, nb + 1)] + [sl_start]

time: 95 us -> 88 us (0.926)
  Pallas kernels: 93.5 us -> 86.5 us
    pallas_call x1, Pallas kernels: 88.6 us -> 81.6 us  [local(): pl.pallas_call(functools.partial(kernel, n, nsp), out_shape=(jax.ShapeDty...]
where the time goes in v4:
time: 88 us; the launch traced here: 87.7 us
  Pallas kernels  86.5 us (98%)
  between operations  1.29 us (1%)
    pallas_call x1, Pallas kernels, local(): pl.pallas_call(functools.partial(kernel, n, nsp), out_shape=(jax.ShapeDty...  81.6 us
    pallas_call x1, Pallas kernels, local(): pl.pallas_call(functools.partial(apply, rows * nsp), out_shape=(jax.Shape...  4.88 us

profile of v4, /device:TPU:0, one launch (start us, length us, event | category | flops | bytes accessed | tf_op | source)
XLA Modules:
  0.0 87.7 jit_solution(1240754104251027397)
XLA Ops:
  1.3 81.6 %shard_map.86 = (bf16[2048,256]{1,0:T(8,128)(2,1)}, bf16[256,2048]{1,0:T(8,128)(2,1)}, f32[256,256]{1,0:T(8,128)}) custom-call(bf16[2048,2048]{1,0:T(8,128)(2,1)} %vals.1, bf16[16,2048]{1,0:T(8,128)(2,1)} %scales.1, bf16[2048,128]{1,0:T(8,128)(2,1)} %slab.1, bf16[16,128]{1,0:T(8,128)(2,1)} %slab_sc.1, bf16[2048,256]{1,0:T(8,128)(2,1)} %test.1, s32[4]{0:T(128)} %owner.1, ...), custom_call_target="tpu_custom_call" | custom-call | flops 5637144576 | bytes 10485760 | tf_op jit(solution)/shard_map/pallas_call | solution.py:428
  82.9 4.9 %shard_map.87 = (bf16[2048,256]{1,0:T(8,128)(2,1)}, f32[256,2048]{1,0:T(8,128)}) custom-call(bf16[2048,256]{1,0:T(8,128)(2,1)} %get-tuple-element.5.sk, bf16[256,2048]{1,0:T(8,128)(2,1)} %get-tuple-element.6.x, f32[256,256]{1,0:T(8,128)} %get-tuple-element.7.inv), custom_call_target="tpu_custom_call" | custom-call | flops 1073741824 | bytes 4194304 | tf_op jit(solution)/shard_map/pallas_call | solution.py:474

commit v5 on v4

--- a/solution.py
+++ b/solution.py
@@ -351,8 +351,9 @@
     g_step(nb)
     g_copy(nb).wait_recv()
 
-    steps = [functools.partial(c_step, i) for i in range(2, nb + 1)] + [sl_start]
-    spots = [(0.5 + i * 1.0 / len(steps), f) for i, f in enumerate(steps)]
+    spots = [
+        (0.5 + 0.65 * (i - 2) / (nb - 2), functools.partial(c_step, i)) for i in range(2, nb + 1)
+    ] + [(1.4, sl_start)]
     early = [(at, f) for at, f in spots if at < 1]
     late = [(at - 1, f) for at, f in spots if at >= 1]
     scale = 1.0 / total_rows

time: 88 us -> 86.9 us (0.988)
  Pallas kernels: 86.5 us -> 85.4 us
    pallas_call x1, Pallas kernels: 81.6 us -> 80.5 us  [local(): pl.pallas_call(functools.partial(kernel, n, nsp), out_shape=(jax.ShapeDty...]
where the time goes in v5:
time: 86.9 us; the launch traced here: 86.7 us
  Pallas kernels  85.4 us (98%)
  between operations  1.29 us (1%)
    pallas_call x1, Pallas kernels, local(): pl.pallas_call(functools.partial(kernel, n, nsp), out_shape=(jax.ShapeDty...  80.5 us
    pallas_call x1, Pallas kernels, local(): pl.pallas_call(functools.partial(apply, rows * nsp), out_shape=(jax.Shape...  4.88 us

profile of v5, /device:TPU:0, one launch (start us, length us, event | category | flops | bytes accessed | tf_op | source)
XLA Modules:
  0.0 86.7 jit_solution(15772558893101850008)
XLA Ops:
  1.3 80.5 %shard_map.86 = (bf16[2048,256]{1,0:T(8,128)(2,1)}, bf16[256,2048]{1,0:T(8,128)(2,1)}, f32[256,256]{1,0:T(8,128)}) custom-call(bf16[2048,2048]{1,0:T(8,128)(2,1)} %vals.1, bf16[16,2048]{1,0:T(8,128)(2,1)} %scales.1, bf16[2048,128]{1,0:T(8,128)(2,1)} %slab.1, bf16[16,128]{1,0:T(8,128)(2,1)} %slab_sc.1, bf16[2048,256]{1,0:T(8,128)(2,1)} %test.1, s32[4]{0:T(128)} %owner.1, ...), custom_call_target="tpu_custom_call" | custom-call | flops 5637144576 | bytes 10485760 | tf_op jit(solution)/shard_map/pallas_call | solution.py:429
  81.8 4.9 %shard_map.87 = (bf16[2048,256]{1,0:T(8,128)(2,1)}, f32[256,2048]{1,0:T(8,128)}) custom-call(bf16[2048,256]{1,0:T(8,128)(2,1)} %get-tuple-element.5.sk, bf16[256,2048]{1,0:T(8,128)(2,1)} %get-tuple-element.6.x, f32[256,256]{1,0:T(8,128)} %get-tuple-element.7.inv), custom_call_target="tpu_custom_call" | custom-call | flops 1073741824 | bytes 4194304 | tf_op jit(solution)/shard_map/pallas_call | solution.py:475
